TPU v7x, 32 devices: a whole 2x2x4 slice. The times are simulated.
32 devices in a mesh: scene: 4 (over z), view: 8 (over y, x, core).
Axes of the slice: x: 2, y: 2, z: 4, core: 2. Of those that a mesh axis runs over, the one named last changes fastest.
Arguments:
- queries: bfloat16 [8192, 1024], P(('scene', 'view')), parts along dimension 0, may hold values from -256 to 256
- keys: bfloat16 [8192, 1024], P(('scene', 'view')), parts along dimension 0, may hold values from -6 to 6
- values: bfloat16 [8192, 1024], P(('scene', 'view')), parts along dimension 0, may hold values from -6 to 6
- grad_out: bfloat16 [8192, 1024], P(('scene', 'view')), parts along dimension 0, may hold values from -6 to 6
- pairs: int32 [64, 4], P(('scene', 'view')), parts along dimension 0, may hold values from 0 to 15, as said below
- counts: int32 [64], P(('scene', 'view')), parts along dimension 0, may hold values from 0 to 4, as said below
Outputs:
- attended: bfloat16 [8192, 1024], P(('scene', 'view')), parts along dimension 0
- grad_queries: bfloat16 [8192, 1024], P(('scene', 'view')), parts along dimension 0
- grad_keys: bfloat16 [8192, 1024], P(('scene', 'view')), parts along dimension 0
- grad_values: bfloat16 [8192, 1024], P(('scene', 'view')), parts along dimension 0
There are 4 independent parts, one for each index of `scene`. A program takes and returns all parts, laid end to end along the dimension named above; each array names one. Nothing has to cross between parts.
Inputs may be any that keep to these rules, and one draw needn't show every extreme that they name: The first counts[v] entries of row v of pairs are distinct blocks at cycle distance 1 or 2 from v; the other entries are blocks of that kind too and are not used. `counts`: some block uses all 4 entries.
All inputs are finite; a program needn't handle non-finite values.
Results may differ from a plain program's by a relative error of at most 0.0078.
Values may be sent and summed in bfloat16 or wider, within the bound.
A program may use at most 64 MiB of HBM per device.

v0:
```python
import jax
import jax.numpy as jnp
from jax import lax
from jax.sharding import PartitionSpec as P

HEADS = 16
HEAD_DIM = 64
VIEW_TOK = 128


masked_score = -1e30


def from_behind(x, axis, by):
    length = lax.axis_size(axis)
    return lax.ppermute(x, axis, [(i, (i + by) % length) for i in range(length)])


def head_split(rows):
    return rows.reshape(rows.shape[0], HEADS, HEAD_DIM)


def block_scores(q_rows, k_rows):
    return jnp.einsum(
        "qhd,khd->hqk", head_split(q_rows), head_split(k_rows), preferred_element_type=jnp.float32
    ) * HEAD_DIM ** (-0.5)


def masked(scores, live):
    return jnp.where(live, scores, masked_score)


def row_stats(scores, live):
    kept = masked(scores, live)
    top = jnp.max(kept, axis=2)
    total = jnp.sum(jnp.exp(kept - top[:, :, None]), axis=2)
    return top + jnp.log(total)


def softmax_rows(scores, live, log_total):
    return jnp.exp(masked(scores, live) - log_total[:, :, None])


def weighted(weights_b, v_rows):
    mixed = jnp.einsum(
        "hqk,khd->qhd", weights_b, head_split(v_rows), preferred_element_type=jnp.float32
    )
    return mixed.reshape(mixed.shape[0], HEADS * HEAD_DIM)


def row_delta(d_rows, out):
    return jnp.sum(head_split(d_rows).astype(jnp.float32) * head_split(out), axis=2).T


def score_grads(q_rows, k_rows, v_rows, d_rows, live, log_total, delta):
    scores = block_scores(q_rows, k_rows)
    weights = softmax_rows(scores, live, log_total)
    prob_grad = jnp.einsum(
        "qhd,khd->hqk", head_split(d_rows), head_split(v_rows), preferred_element_type=jnp.float32
    )
    score_grad = (weights * (prob_grad - delta[:, :, None])).astype(jnp.bfloat16)
    return (weights.astype(jnp.bfloat16), score_grad)


def query_grad(score_grad, k_rows):
    result = jnp.einsum(
        "hqk,khd->qhd", score_grad, head_split(k_rows), preferred_element_type=jnp.float32
    ) * HEAD_DIM ** (-0.5)
    return result.reshape(result.shape[0], HEADS * HEAD_DIM)


def key_grads(weights_b, score_grad, q_rows, d_rows):
    key_part = jnp.einsum(
        "hqk,qhd->khd", score_grad, head_split(q_rows), preferred_element_type=jnp.float32
    ) * HEAD_DIM ** (-0.5)
    value_part = jnp.einsum(
        "hqk,qhd->khd", weights_b, head_split(d_rows), preferred_element_type=jnp.float32
    )
    width = HEADS * HEAD_DIM
    return jnp.stack(
        [key_part.reshape(key_part.shape[0], width), value_part.reshape(value_part.shape[0], width)]
    )


def body(queries, keys, values, grad_out, pairs, counts):
    view_rows = VIEW_TOK
    local_views = queries.shape[0] // view_rows
    views = local_views * lax.axis_size("view")
    first_view = lax.axis_index("view") * local_views
    own_views = first_view + jnp.arange(local_views, dtype=jnp.int32)
    relative = (pairs - own_views[:, None] + views // 2) % views - views // 2
    slot_live = jnp.arange(pairs.shape[1], dtype=jnp.int32)[None, :] < counts[:, None]
    offsets = jnp.arange(-2, 3, dtype=jnp.int32)
    allowed = (
        jnp.any((relative[:, :, None] == offsets[None, None, :]) & slot_live[:, :, None], axis=1)
        | (offsets == 0)[None, :]
    )
    local_kv = jnp.stack([keys, values])
    fetched = [from_behind(local_kv, "view", step) for step in (1, -1)]
    window_kv = jnp.concatenate([fetched[0], local_kv, fetched[1]], axis=1)
    span = local_views * view_rows
    outs, log_totals, deltas = ([], [], [])
    for view in range(local_views):
        q_rows = queries[view * view_rows : (view + 1) * view_rows]
        d_rows = grad_out[view * view_rows : (view + 1) * view_rows]
        k_rows = window_kv[0, view * view_rows : (view + 5) * view_rows]
        v_rows = window_kv[1, view * view_rows : (view + 5) * view_rows]
        live = jnp.repeat(allowed[view], view_rows)[None, None, :]
        scores = block_scores(q_rows, k_rows)
        log_total = row_stats(scores, live)
        out = weighted(softmax_rows(scores, live, log_total).astype(jnp.bfloat16), v_rows)
        outs.append(out)
        log_totals.append(log_total)
        deltas.append(row_delta(d_rows, out))
    attended = jnp.concatenate(outs, axis=0).astype(jnp.bfloat16)
    again = [from_behind(local_kv, "view", step) for step in (1, -1)]
    back_kv = jnp.concatenate([again[0], local_kv, again[1]], axis=1)
    grad_window = jnp.zeros((2, 3 * span, HEADS * HEAD_DIM), jnp.float32)
    query_parts = []
    for view in range(local_views):
        q_rows = queries[view * view_rows : (view + 1) * view_rows]
        d_rows = grad_out[view * view_rows : (view + 1) * view_rows]
        log_total = log_totals[view]
        delta = deltas[view]
        k_rows = back_kv[0, view * view_rows : (view + 5) * view_rows]
        v_rows = back_kv[1, view * view_rows : (view + 5) * view_rows]
        live = jnp.repeat(allowed[view], view_rows)[None, None, :]
        weights_b, score_grad = score_grads(q_rows, k_rows, v_rows, d_rows, live, log_total, delta)
        query_parts.append(query_grad(score_grad, k_rows))
        grad_window = grad_window.at[:, view * view_rows : (view + 5) * view_rows].add(
            key_grads(weights_b, score_grad, q_rows, d_rows)
        )
    grad_queries = jnp.concatenate(query_parts, axis=0).astype(jnp.bfloat16)
    returned = [
        from_behind(grad_window[:, begin : begin + span], "view", step)
        for begin, step in ((0, -1), (2 * span, 1))
    ]
    key_sums = grad_window[:, span : 2 * span] + returned[0] + returned[1]
    grad_keys = key_sums[0].astype(jnp.bfloat16)
    grad_values = key_sums[1].astype(jnp.bfloat16)
    return (attended, grad_queries, grad_keys, grad_values)


def solution(mesh):
    placed = (
        P(("scene", "view"), None),
        P(("scene", "view"), None),
        P(("scene", "view"), None),
        P(("scene", "view"), None),
        P(("scene", "view"), None),
        P(("scene", "view")),
    )
    return jax.shard_map(
        body,
        mesh=mesh,
        in_specs=placed,
        out_specs=(
            P(("scene", "view"), None),
            P(("scene", "view"), None),
            P(("scene", "view"), None),
            P(("scene", "view"), None),
        ),
        check_vma=False,
    )
```

profile of v0, /device:TPU:0, one launch (start us, length us, event | category | flops | bytes accessed | tf_op | source)
XLA Modules:
  0.0 147.3 jit_solution(18433097820484747466)
XLA Ops:
  0.7 1.4 pad_maximum_fusion.1
  2.1 3.4 %collective-permute-start.1 = (bf16[2,256,1024]{2,1,0:T(8,128)(2,1)S(1)}, bf16[2,256,1024]{2,1,0:T(8,128)(2,1)}, u32[]{:S(2)}, u32[]{:S(2)}) collective-permute-start(bf16[2,256,1024]{2,1,0:T(8,128)(2,1)S(1)} %pad_maximum_fusion.1), channel_id=1, source_target_pairs={{0,7},{1,0},{2,1},{3,2},{4,3},{5,4},{6,5},{7,6},{8,15},{9,8},{10,9... | collective-permute-start | bytes 3145736 | tf_op jit(solution)/shard_map/ppermute | solution.py:16
  5.5 0.7 iota_compare_fusion.1
  6.2 1.8 %fusion.24 = (bf16[128,1024]{1,0:T(8,128)(2,1)S(1)}, bf16[128,1024]{1,0:T(8,128)(2,1)}) fusion(bf16[256,1024]{1,0:T(8,128)(2,1)} %param.10), kind=kLoop, calls=%fused_computation.64 | loop fusion | bytes 1048576 | tf_op jit(solution)/shard_map/slice | solution.py:104
  7.9 1.1 fusion.23
  9.2 1.1 copy.40
  10.3 0.8 copy.44
  11.2 0.8 copy.46
  12.3 15.8 %collective-permute-done.1 = bf16[2,256,1024]{2,1,0:T(8,128)(2,1)} collective-permute-done((bf16[2,256,1024]{2,1,0:T(8,128)(2,1)S(1)}, bf16[2,256,1024]{2,1,0:T(8,128)(2,1)}, u32[]{:S(2)}, u32[]{:S(2)}) %collective-permute-start.1) | collective-permute-done | bytes 1048608 | tf_op jit(solution)/shard_map/ppermute | solution.py:16
  28.1 2.0 %collective-permute-done = bf16[2,256,1024]{2,1,0:T(8,128)(2,1)} collective-permute-done((bf16[2,256,1024]{2,1,0:T(8,128)(2,1)S(1)}, bf16[2,256,1024]{2,1,0:T(8,128)(2,1)}, u32[]{:S(2)}, u32[]{:S(2)}) %collective-permute-start) | collective-permute-done | bytes 1048608 | tf_op jit(solution)/shard_map/ppermute | solution.py:16
  30.1 1.8 %pad_maximum_fusion = bf16[2,768,1024]{2,1,0:T(8,128)(2,1)S(1)} fusion(bf16[2,256,1024]{2,1,0:T(8,128)(2,1)} %collective-permute-done.1, bf16[1,256,1024]{2,1,0:T(8,128)(2,1)S(1)} %bitcast.127, bf16[1,256,1024]{2,1,0:T(8,128)(2,1)S(1)} %bitcast.129, bf16[2,256,1024]{2,1,0:T(8,128)(2,1)} %collective-permute-done), kind=kLoop, calls=%fused_computation.23 | loop fusion | flops 12582912 | bytes 6291456 | tf_op jit(solution)/shard_map/concatenate | solution.py:100
  31.9 2.1 %fusion.22 = (bf16[1,640,1024]{2,1,0:T(8,128)(2,1)S(1)}, bf16[1,640,1024]{2,1,0:T(8,128)(2,1)}, bf16[1,640,1024]{2,1,0:T(8,128)(2,1)}, bf16[1,640,1024]{2,1,0:T(8,128)(2,1)}) fusion(bf16[2,768,1024]{2,1,0:T(8,128)(2,1)S(1)} %pad_maximum_fusion), kind=kLoop, calls=%fused_computation.62 | loop fusion | bytes 10485760 | tf_op jit(solution)/shard_map/slice | solution.py:106
  34.7 1.7 %copy.39 = bf16[1,640,1024]{1,2,0:T(8,128)(2,1)S(1)} copy(bf16[1,640,1024]{2,1,0:T(8,128)(2,1)} %get-tuple-element.31) | data formatting | bytes 2621440 | tf_op jit(solution)/shard_map/slice | solution.py:106
  36.4 2.4 %copy.38 = bf16[1,640,1024]{1,2,0:T(8,128)(2,1)} copy(bf16[1,640,1024]{2,1,0:T(8,128)(2,1)} %get-tuple-element.32) | data formatting | bytes 2621440 | tf_op jit(solution)/shard_map/slice | solution.py:107
  38.8 2.4 %copy.34 = bf16[1,640,1024]{1,2,0:T(8,128)(2,1)} copy(bf16[1,640,1024]{2,1,0:T(8,128)(2,1)} %get-tuple-element.33) | data formatting | bytes 2621440 | tf_op jit(solution)/shard_map/slice | solution.py:107
  41.2 1.3 bitcast_reduce_fusion
  42.6 1.1 fusion.3
  43.8 2.3 %multiply_reduce_fusion = (f32[128,16]{0,1:T(8,128)S(1)}, bf16[128,16,64]{0,2,1:T(8,128)(2,1)}) fusion(bf16[128,1024]{0,1:T(8,128)(2,1)S(1)} %copy-done.8, bf16[640,16,64]{0,2,1:T(8,128)(2,1)S(1)} %bitcast.132, f32[16,640,128]{2,1,0:T(8,128)S(1)} %get-tuple-element.47, f32[16,128]{1,0:T(8,128)S(1)} %log_add_fusion, pred[640]{0:T(1024)(128)(4,1)S(1)} %get-tuple-element.52), kind=kOutput, calls=%fused_computation.40 | convolution fusion | flops 173537280 | bytes 7094912 | tf_op jit(solution)/shard_map/hqk,khd->qhd/dot_general | solution.py:45
  46.0 3.0 %fusion.16 = f32[16,640,64]{1,2,0:T(8,128)} fusion(bf16[128,16,64]{0,2,1:T(8,128)(2,1)S(1)} %bitcast.136, f32[16,640,128]{2,1,0:T(8,128)S(1)} %get-tuple-element.47, f32[16,128]{1,0:T(8,128)S(1)} %log_add_fusion, pred[640]{0:T(1024)(128)(4,1)S(1)} %get-tuple-element.52), kind=kOutput, calls=%fused_computation.60 | convolution fusion | flops 173015040 | bytes 8135296 | tf_op jit(solution)/shard_map/hqk,qhd->khd/dot_general | solution.py:76
  49.0 2.1 %fusion = bf16[16,128,640]{1,2,0:T(8,128)(2,1)S(1)} fusion(f32[16,640,128]{2,1,0:T(8,128)S(1)} %get-tuple-element.47, f32[16,128]{1,0:T(8,128)S(1)} %bitcast.142, f32[16,128]{1,0:T(8,128)S(1)} %log_add_fusion, pred[640]{0:T(1024)(128)(4,1)S(1)} %get-tuple-element.52, bf16[640,16,64]{0,2,1:T(8,128)(2,1)S(1)} %bitcast.133, bf16[128,16,64]{0,2,1:T(8,128)(2,1)S(1)} %bitcast.137), kind=kOutput, calls=%fused_computation.4 | convolution fusion | flops 175636480 | bytes 9454208 | tf_op jit(solution)/shard_map/qhd,khd->hqk/dot_general | solution.py:58
  51.2 1.5 %copy-done.1 = bf16[16,128,640]{1,2,0:T(8,128)(2,1)} copy-done((bf16[16,128,640]{1,2,0:T(8,128)(2,1)}, bf16[16,128,640]{1,2,0:T(8,128)(2,1)S(1)}, u32[]{:S(2)}) %copy-start.1) | copy-done | bytes 2621464
  52.7 2.7 %convolution_multiply_fusion = f32[16,640,64]{1,2,0:T(8,128)} fusion(bf16[16,128,640]{1,2,0:T(8,128)(2,1)S(1)} %fusion, bf16[128,16,64]{0,2,1:T(8,128)(2,1)S(1)} %bitcast.125), kind=kOutput, calls=%fused_computation.27 | convolution fusion | flops 168427520 | bytes 5505024 | tf_op jit(solution)/shard_map/hqk,qhd->khd/dot_general | solution.py:73
  55.3 3.2 %copy.56 = f32[1,640,1024]{2,1,0:T(8,128)} copy(f32[1,640,1024]{1,2,0:T(8,128)} %bitcast.120) | data formatting | bytes 5242880 | tf_op jit(solution)/shard_map/stack;reshape | solution.py:80
  58.5 3.2 %copy.57 = f32[1,640,1024]{2,1,0:T(8,128)} copy(f32[1,640,1024]{1,2,0:T(8,128)} %bitcast.118) | data formatting | bytes 5242880 | tf_op jit(solution)/shard_map/stack;reshape | solution.py:80
  61.8 1.3 bitcast_reduce_fusion.1
  63.1 1.1 fusion.6
  64.3 2.3 %multiply_reduce_fusion.1 = (f32[128,16]{0,1:T(8,128)S(1)}, bf16[128,16,64]{0,2,1:T(8,128)(2,1)}) fusion(bf16[128,1024]{0,1:T(8,128)(2,1)S(1)} %copy-done.7, bf16[640,16,64]{0,2,1:T(8,128)(2,1)S(1)} %bitcast.130, f32[16,640,128]{2,1,0:T(8,128)S(1)} %get-tuple-element.50, f32[16,128]{1,0:T(8,128)S(1)} %log_add_fusion.1, pred[640]{0:T(1024)(128)(4,1)S(1)} %get-tuple-element.53), kind=kOutput, calls=%fused_computation.41 | convolution fusion | flops 173537280 | bytes 7094912 | tf_op jit(solution)/shard_map/hqk,khd->qhd/dot_general | solution.py:45
  66.5 3.0 %fusion.19 = f32[16,640,64]{1,2,0:T(8,128)} fusion(bf16[128,16,64]{0,2,1:T(8,128)(2,1)S(1)} %bitcast.134, f32[16,640,128]{2,1,0:T(8,128)S(1)} %get-tuple-element.50, f32[16,128]{1,0:T(8,128)S(1)} %log_add_fusion.1, pred[640]{0:T(1024)(128)(4,1)S(1)} %get-tuple-element.53), kind=kOutput, calls=%fused_computation.61 | convolution fusion | flops 173015040 | bytes 8135296 | tf_op jit(solution)/shard_map/hqk,qhd->khd/dot_general | solution.py:76
  69.5 2.1 %fusion.1 = bf16[16,128,640]{1,2,0:T(8,128)(2,1)S(1)} fusion(f32[16,640,128]{2,1,0:T(8,128)S(1)} %get-tuple-element.50, f32[16,128]{1,0:T(8,128)S(1)} %bitcast.143, f32[16,128]{1,0:T(8,128)S(1)} %log_add_fusion.1, pred[640]{0:T(1024)(128)(4,1)S(1)} %get-tuple-element.53, bf16[640,16,64]{0,2,1:T(8,128)(2,1)S(1)} %bitcast.131, ...), kind=kOutput, calls=%fused_computation.6 | convolution fusion | flops 175636480 | bytes 9454208 | tf_op jit(solution)/shard_map/qhd,khd->hqk/dot_general | solution.py:58
  71.7 1.5 %copy-done.2 = bf16[16,128,640]{1,2,0:T(8,128)(2,1)} copy-done((bf16[16,128,640]{1,2,0:T(8,128)(2,1)}, bf16[16,128,640]{1,2,0:T(8,128)(2,1)S(1)}, u32[]{:S(2)}) %copy-start.2) | copy-done | bytes 2621464
  73.2 2.6 %convolution_multiply_fusion.1 = f32[16,640,64]{1,2,0:T(8,128)} fusion(bf16[16,128,640]{1,2,0:T(8,128)(2,1)S(1)} %fusion.1, bf16[128,16,64]{0,2,1:T(8,128)(2,1)S(1)} %bitcast.123), kind=kOutput, calls=%fused_computation.28 | convolution fusion | flops 168427520 | bytes 5505024 | tf_op jit(solution)/shard_map/hqk,qhd->khd/dot_general | solution.py:73
  75.8 3.2 %copy.52 = f32[1,640,1024]{2,1,0:T(8,128)} copy(f32[1,640,1024]{1,2,0:T(8,128)} %bitcast.121) | data formatting | bytes 5242880 | tf_op jit(solution)/shard_map/stack;reshape | solution.py:80
  79.1 3.3 %copy.53 = f32[1,640,1024]{2,1,0:T(8,128)} copy(f32[1,640,1024]{1,2,0:T(8,128)} %bitcast.119) | data formatting | bytes 5242880 | tf_op jit(solution)/shard_map/stack;reshape | solution.py:80
  82.3 3.1 %select_maximum_fusion = f32[2,768,1024]{2,1,0:T(8,128)S(1)} fusion(f32[1,640,1024]{2,1,0:T(8,128)} %copy.53, f32[1,640,1024]{2,1,0:T(8,128)} %copy.52), kind=kLoop, calls=%fused_computation | loop fusion | flops 6291456 | bytes 11534336 | tf_op jit(solution)/shard_map/stack | solution.py:80
  85.4 4.6 %constant_dynamic-update-slice_fusion = (f32[2,768,1024]{2,1,0:T(8,128)S(1)}, f32[2,640,1024]{2,1,0:T(8,128)S(1)}) fusion(f32[2,768,1024]{2,1,0:T(8,128)S(1)} %select_maximum_fusion, f32[1,640,1024]{2,1,0:T(8,128)} %copy.57, f32[1,640,1024]{2,1,0:T(8,128)} %copy.56), kind=kLoop, calls=%fused_computation.56 | loop fusion | flops 2621440 | bytes 20971520 | tf_op jit(solution)/shard_map/scatter-add | solution.py:130
  90.1 1.6 %slice.126 = f32[2,256,1024]{2,1,0:T(8,128)} slice(f32[2,768,1024]{2,1,0:T(8,128)S(1)} %get-tuple-element.28), slice={[0:2], [0:256], [0:1024]} | slice | bytes 4194304 | tf_op jit(solution)/shard_map/slice | solution.py:135
  91.7 1.3 copy-done
  93.0 1.5 slice.127
  94.5 2.6 %collective-permute-start.2 = (f32[2,256,1024]{2,1,0:T(8,128)}, f32[2,256,1024]{2,1,0:T(8,128)}, u32[]{:S(2)}, u32[]{:S(2)}) collective-permute-start(f32[2,256,1024]{2,1,0:T(8,128)} %slice.126), channel_id=1, source_target_pairs={{0,7},{1,0},{2,1},{3,2},{4,3},{5,4},{6,5},{7,6},{8,15},{9,8},{10,9... | collective-permute-start | bytes 6291464 | tf_op jit(solution)/shard_map/ppermute | solution.py:16
  97.1 1.1 copy.43
  98.2 2.4 %fusion.13 = bf16[16,64,128]{2,1,0:T(8,128)(2,1)S(1)} fusion(bf16[640,16,64]{0,2,1:T(8,128)(2,1)S(1)} %bitcast.117, bf16[16,128,640]{1,2,0:T(8,128)(2,1)} %copy-done.1), kind=kOutput, calls=%fused_computation.34 | convolution fusion | flops 168034304 | bytes 4194304 | tf_op jit(solution)/shard_map/hqk,khd->qhd/dot_general | solution.py:66
  100.8 1.1 copy.42
  101.9 2.4 %fusion.12 = bf16[16,64,128]{2,1,0:T(8,128)(2,1)S(1)} fusion(bf16[640,16,64]{0,2,1:T(8,128)(2,1)S(1)} %bitcast.115, bf16[16,128,640]{1,2,0:T(8,128)(2,1)} %copy-done.2), kind=kOutput, calls=%fused_computation.33 | convolution fusion | flops 168034304 | bytes 4194304 | tf_op jit(solution)/shard_map/hqk,khd->qhd/dot_general | solution.py:66
  104.4 0.8 pad_maximum_fusion.2
  105.2 0.8 pad_maximum_fusion.3
  106.1 36.8 %collective-permute-done.3 = f32[2,256,1024]{2,1,0:T(8,128)} collective-permute-done((f32[2,256,1024]{2,1,0:T(8,128)}, f32[2,256,1024]{2,1,0:T(8,128)}, u32[]{:S(2)}, u32[]{:S(2)}) %collective-permute-start.3) | collective-permute-done | bytes 2097184 | tf_op jit(solution)/shard_map/ppermute | solution.py:16
  142.8 3.4 %fusion.11 = bf16[2,256,1024]{2,1,0:T(8,128)(2,1)S(1)} fusion(f32[2,256,1024]{2,1,0:T(8,128)} %collective-permute-done.3, f32[2,256,1024]{2,1,0:T(8,128)} %collective-permute-done.2, f32[2,640,1024]{2,1,0:T(8,128)} %copy-done), kind=kLoop, calls=%fused_computation.26 | loop fusion | flops 1572864 | bytes 7340032 | tf_op jit(solution)/shard_map/convert.1
  146.3 1.0 slice_bitcast_fusion
  (34 shorter events, 1.5 us)
Async XLA Ops:
  0.6 29.5 %copy-start.3 = (bf16[256,1024]{1,0:T(8,128)(2,1)S(1)}, bf16[256,1024]{1,0:T(8,128)(2,1)}, u32[]{:S(2)}) copy-start(bf16[256,1024]{1,0:T(8,128)(2,1)} %param.12) | copy-start | bytes 1572868
  0.6 29.5 %copy-start.4 = (bf16[256,1024]{1,0:T(8,128)(2,1)S(1)}, bf16[256,1024]{1,0:T(8,128)(2,1)}, u32[]{:S(2)}) copy-start(bf16[256,1024]{1,0:T(8,128)(2,1)} %param.11) | copy-start | bytes 1572868
  0.7 11.4 %copy-start.9 = (s32[2,4]{1,0:T(2,128)S(1)}, s32[2,4]{1,0:T(2,128)}, u32[]{:S(2)}) copy-start(s32[2,4]{1,0:T(2,128)} %param.14) | copy-start | bytes 100
  2.1 26.0 %collective-permute-start.1 = (bf16[2,256,1024]{2,1,0:T(8,128)(2,1)S(1)}, bf16[2,256,1024]{2,1,0:T(8,128)(2,1)}, u32[]{:S(2)}, u32[]{:S(2)}) collective-permute-start(bf16[2,256,1024]{2,1,0:T(8,128)(2,1)S(1)} %pad_maximum_fusion.1), channel_id=1, source_target_pairs={{0,7},{1,0},{2,1},{3,2},{4,3},{5,4},{6,5},{7,6},{8,15},{9,8},{10,9... | collective-permute-start | bytes 3145736 | tf_op jit(solution)/shard_map/ppermute | solution.py:16
  5.4 24.7 %collective-permute-start = (bf16[2,256,1024]{2,1,0:T(8,128)(2,1)S(1)}, bf16[2,256,1024]{2,1,0:T(8,128)(2,1)}, u32[]{:S(2)}, u32[]{:S(2)}) collective-permute-start(bf16[2,256,1024]{2,1,0:T(8,128)(2,1)S(1)} %pad_maximum_fusion.1), channel_id=1, source_target_pairs={{0,1},{1,2},{2,3},{3,4},{4,5},{5,6},{6,7},{7,0},{8,9},{9,10},{10,1... | collective-permute-start | bytes 3145736 | tf_op jit(solution)/shard_map/ppermute | solution.py:16
  41.2 2.5 %copy-start.6 = (bf16[1,640,1024]{1,2,0:T(8,128)(2,1)S(1)}, bf16[1,640,1024]{1,2,0:T(8,128)(2,1)}, u32[]{:S(2)}) copy-start(bf16[1,640,1024]{1,2,0:T(8,128)(2,1)} %copy.38) | copy-start | bytes 3932164
  41.2 2.5 %copy-start.8 = (bf16[128,1024]{0,1:T(8,128)(2,1)S(1)}, bf16[128,1024]{0,1:T(8,128)(2,1)}, u32[]{:S(2)}) copy-start(bf16[128,1024]{0,1:T(8,128)(2,1)} %copy.46) | copy-start | bytes 786436
  51.2 1.5 %copy-start.1 = (bf16[16,128,640]{1,2,0:T(8,128)(2,1)}, bf16[16,128,640]{1,2,0:T(8,128)(2,1)S(1)}, u32[]{:S(2)}) copy-start(bf16[16,128,640]{1,2,0:T(8,128)(2,1)S(1)} %fusion) | copy-start | bytes 7864324
  61.8 2.5 %copy-start.5 = (bf16[1,640,1024]{1,2,0:T(8,128)(2,1)S(1)}, bf16[1,640,1024]{1,2,0:T(8,128)(2,1)}, u32[]{:S(2)}) copy-start(bf16[1,640,1024]{1,2,0:T(8,128)(2,1)} %copy.34) | copy-start | bytes 3932164
  61.8 2.5 %copy-start.7 = (bf16[128,1024]{0,1:T(8,128)(2,1)S(1)}, bf16[128,1024]{0,1:T(8,128)(2,1)}, u32[]{:S(2)}) copy-start(bf16[128,1024]{0,1:T(8,128)(2,1)} %copy.44) | copy-start | bytes 786436
  71.7 1.5 %copy-start.2 = (bf16[16,128,640]{1,2,0:T(8,128)(2,1)}, bf16[16,128,640]{1,2,0:T(8,128)(2,1)S(1)}, u32[]{:S(2)}) copy-start(bf16[16,128,640]{1,2,0:T(8,128)(2,1)S(1)} %fusion.1) | copy-start | bytes 7864324
  90.1 3.0 %copy-start = (f32[2,640,1024]{2,1,0:T(8,128)}, f32[2,640,1024]{2,1,0:T(8,128)S(1)}, u32[]{:S(2)}) copy-start(f32[2,640,1024]{2,1,0:T(8,128)S(1)} %get-tuple-element.29) | copy-start | bytes 15728644
  94.5 48.4 %collective-permute-start.3 = (f32[2,256,1024]{2,1,0:T(8,128)}, f32[2,256,1024]{2,1,0:T(8,128)}, u32[]{:S(2)}, u32[]{:S(2)}) collective-permute-start(f32[2,256,1024]{2,1,0:T(8,128)} %slice.127), channel_id=1, source_target_pairs={{0,1},{1,2},{2,3},{3,4},{4,5},{5,6},{6,7},{7,0},{8,9},{9,10},{10,1... | collective-permute-start | bytes 6291464 | tf_op jit(solution)/shard_map/ppermute | solution.py:16
  94.5 48.4 %collective-permute-start.2 = (f32[2,256,1024]{2,1,0:T(8,128)}, f32[2,256,1024]{2,1,0:T(8,128)}, u32[]{:S(2)}, u32[]{:S(2)}) collective-permute-start(f32[2,256,1024]{2,1,0:T(8,128)} %slice.126), channel_id=1, source_target_pairs={{0,7},{1,0},{2,1},{3,2},{4,3},{5,4},{6,5},{7,6},{8,15},{9,8},{10,9... | collective-permute-start | bytes 6291464 | tf_op jit(solution)/shard_map/ppermute | solution.py:16
where the time goes:
time: 148 us; the launch traced here: 147 us
  waiting for transfers between devices  54.6 us (37%)
  local copies, waits for them, and re-layouts  39.1 us (26%)
  matrix products  27.5 us (19%)
  other arithmetic  19.1 us (13%)
  starting transfers between devices  6.03 us (4%)
    ppermute x4, waiting for transfers between devices, from_behind(): lax.ppermute(x, axis, [(i, (i + by) % length) for i in range(length)])  54.6 us
    another operation x4, local copies, waits for them, and re-layouts, key_grads(): jnp.stack([key_part.reshape(key_part.shape[0], width), value_part.reshape...  12.9 us
    ppermute x4, starting transfers between devices, from_behind(): lax.ppermute(x, axis, [(i, (i + by) % length) for i in range(length)])  6.03 us
    dot_general x2, matrix products, key_grads(): jnp.einsum('hqk,qhd->khd', weights_b, head_split(d_rows), preferred_eleme...  5.97 us
    dot_general x2, matrix products, key_grads(): jnp.einsum('hqk,qhd->khd', score_grad, head_split(q_rows), preferred_elem...  5.3 us
    slice x2, local copies, waits for them, and re-layouts, body(): v_rows = window_kv[1, view * view_rows:(view + 5) * view_rows]  4.84 us
    dot_general x2, matrix products, query_grad(): jnp.einsum('hqk,khd->qhd', score_grad, head_split(k_rows), preferred_elem...  4.78 us
    scatter-add x1, other arithmetic, body(): grad_window.at[:, view * view_rows:(view + 5) * view_rows]  4.61 us
  transfers between devices with their start and end apart: 4, of which 3 were waited for; matrix products, arithmetic and copies ran while one was open for 11% of the time, Pallas kernels for 0%

commit v1 on v0

v1 whole, which is shorter than its diff:
```python
import jax
import jax.numpy as jnp
from jax import lax
from jax.experimental import pallas as pl
from jax.experimental.pallas import tpu as pltpu
from jax.sharding import PartitionSpec as P

HEAD_DIM = 64
VIEW_TOK = 128
LANES = 2 * HEAD_DIM
MASKED = -1e30
REACH = 2


def nt(a, b):
    return lax.dot_general(a, b, (((1,), (1,)), ((), ())), preferred_element_type=jnp.float32)


def tn(a, b):
    return lax.dot_general(a, b, (((0,), (0,)), ((), ())), preferred_element_type=jnp.float32)


def nn(a, b):
    return jnp.dot(a, b, preferred_element_type=jnp.float32)


def two_heads(rows):
    first = lax.broadcasted_iota(jnp.int32, rows.shape, 1) < HEAD_DIM
    zero = jnp.zeros_like(rows)
    return jnp.concatenate([jnp.where(first, rows, zero), jnp.where(first, zero, rows)], axis=0)


def fold_heads(wide):
    first = lax.broadcasted_iota(jnp.int32, (LANES, VIEW_TOK), 0) < HEAD_DIM
    return jnp.where(first, wide[:, :VIEW_TOK], wide[:, VIEW_TOK:])


def block_bias(pairs, counts, view, own, views, offset):
    target = lax.rem(own + offset + views, views)
    live = jnp.bool_(False)
    for slot in range(pairs.shape[1]):
        live = live | ((pairs[view, slot] == target) & (slot < counts[view]))
    return jnp.where(live, 0.0, MASKED).astype(jnp.float32)


def attend(q, d, k_win, v_win, biases):
    qs = two_heads((q.astype(jnp.float32) * HEAD_DIM ** -0.5).astype(jnp.bfloat16))
    ds = two_heads(d)
    scores = nt(k_win, qs)
    tiles = []
    for j, bias in enumerate(biases):
        tile = scores[j * VIEW_TOK : (j + 1) * VIEW_TOK]
        tiles.append(tile if bias is None else tile + bias)
    scores = jnp.concatenate(tiles, axis=0)
    grown = jnp.exp(scores - jnp.max(scores, axis=0, keepdims=True))
    weights = grown * (1.0 / jnp.sum(grown, axis=0, keepdims=True))
    weights_b = weights.astype(jnp.bfloat16)
    out = fold_heads(tn(v_win, weights_b))
    product = out * d.astype(jnp.float32).T
    delta = jnp.concatenate(
        [
            jnp.sum(product[:HEAD_DIM], axis=0, keepdims=True),
            jnp.sum(product[HEAD_DIM:], axis=0, keepdims=True),
        ],
        axis=1,
    )
    score_grad = (weights * (nt(v_win, ds) - delta)).astype(jnp.bfloat16)
    grad_q = fold_heads(tn(k_win, score_grad)) * HEAD_DIM ** -0.5
    return (
        out.T.astype(jnp.bfloat16),
        grad_q.T.astype(jnp.bfloat16),
        nn(score_grad, qs),
        nn(weights_b, ds),
    )


def kernel(
    size, chunks,
    pairs, counts, q_ref, k_ref, v_ref, d_ref,
    a_ref, gq_ref, gk_ref, gv_ref,
    k_in, v_in, g_out, g_in, own_k, own_v,
    kv_send, kv_recv, g_send, g_recv,
):
    me = lax.axis_index("view")
    peers = (lax.rem(me + size - 1, size), lax.rem(me + 1, size))
    span = q_ref.shape[0]
    local_views = span // VIEW_TOK
    views = size * local_views

    barrier = pltpu.get_barrier_semaphore()
    for peer in peers:
        pl.semaphore_signal(
            barrier, inc=1, device_id={"view": peer}, device_id_type=pl.DeviceIdType.MESH
        )
    pl.semaphore_wait(barrier, 2)

    def columns(c):
        return pl.ds(pl.multiple_of(c * LANES, LANES), LANES)

    def kv_copy(c, side, which):
        src, dst = ((k_ref, k_in), (v_ref, v_in))[which]
        return pltpu.make_async_remote_copy(
            src_ref=src.at[:, columns(c)],
            dst_ref=dst.at[1 - side, c],
            send_sem=kv_send.at[side, which, c],
            recv_sem=kv_recv.at[1 - side, which, c],
            device_id={"view": peers[side]},
            device_id_type=pl.DeviceIdType.MESH,
        )

    def grad_copy(c, side):
        return pltpu.make_async_remote_copy(
            src_ref=g_out.at[side, c],
            dst_ref=g_in.at[1 - side, c],
            send_sem=g_send.at[side, c],
            recv_sem=g_recv.at[1 - side, c],
            device_id={"view": peers[side]},
            device_id_type=pl.DeviceIdType.MESH,
        )

    def send_all(c, _):
        for which in (0, 1):
            for side in (0, 1):
                kv_copy(c, side, which).start()
        return 0

    lax.fori_loop(0, chunks, send_all, 0)

    biases = []
    for view in range(local_views):
        own = me * local_views + view
        biases.append(
            [
                None if offset == 0 else block_bias(pairs, counts, view, own, views, offset)
                for offset in range(-REACH, REACH + 1)
            ]
        )

    def work(c, _):
        for which in (0, 1):
            for side in (0, 1):
                kv_copy(c, side, which).wait_recv()
        cols = columns(c)
        k_all = jnp.concatenate([k_in[0, c], k_ref[:, cols], k_in[1, c]], axis=0)
        v_all = jnp.concatenate([v_in[0, c], v_ref[:, cols], v_in[1, c]], axis=0)
        sums = [[None] * (3 * local_views), [None] * (3 * local_views)]
        for view in range(local_views):
            rows = slice(view * VIEW_TOK, (view + 1) * VIEW_TOK)
            base = local_views + view - REACH
            win = slice(base * VIEW_TOK, (base + 2 * REACH + 1) * VIEW_TOK)
            out, grad_q, part_k, part_v = attend(
                q_ref[rows, cols], d_ref[rows, cols], k_all[win], v_all[win], biases[view]
            )
            a_ref[rows, cols] = out
            gq_ref[rows, cols] = grad_q
            for total, part in zip(sums, (part_k, part_v)):
                for j in range(2 * REACH + 1):
                    tile = part[j * VIEW_TOK : (j + 1) * VIEW_TOK]
                    at = base + j
                    total[at] = tile if total[at] is None else total[at] + tile
        for which, (total, kept) in enumerate(zip(sums, (own_k, own_v))):
            for j in range(local_views):
                rows = slice(j * VIEW_TOK, (j + 1) * VIEW_TOK)
                g_out[0, c, which, rows] = total[j].astype(jnp.bfloat16)
                g_out[1, c, which, rows] = total[2 * local_views + j].astype(jnp.bfloat16)
                kept[c, rows] = total[local_views + j]
        for side in (0, 1):
            grad_copy(c, side).start()
        return 0

    lax.fori_loop(0, chunks, work, 0)

    def finish(c, _):
        cols = columns(c)
        for side in (0, 1):
            grad_copy(c, side).wait_recv()
        for which, (kept, result) in enumerate(((own_k, gk_ref), (own_v, gv_ref))):
            total = (
                kept[c]
                + g_in[0, c, which].astype(jnp.float32)
                + g_in[1, c, which].astype(jnp.float32)
            )
            result[:, cols] = total.astype(jnp.bfloat16)
        return 0

    lax.fori_loop(0, chunks, finish, 0)

    def drain(c, _):
        for side in (0, 1):
            for which in (0, 1):
                kv_copy(c, side, which).wait_send()
            grad_copy(c, side).wait_send()
        return 0

    lax.fori_loop(0, chunks, drain, 0)


def body(queries, keys, values, grad_out, pairs, counts):
    size = lax.axis_size("view")
    span, width = queries.shape
    chunks = width // LANES
    assert span == REACH * VIEW_TOK
    vmem = pl.BlockSpec(memory_space=pltpu.VMEM)
    smem = pl.BlockSpec(memory_space=pltpu.SMEM)

    def run(*refs):
        kernel(size, chunks, *refs)

    pair_flops = 2 * 6 * 2 * 2 * VIEW_TOK * 5 * VIEW_TOK * LANES
    return pl.pallas_call(
        run,
        name="windowed_attention",
        out_shape=[jax.ShapeDtypeStruct((span, width), jnp.bfloat16)] * 4,
        in_specs=[smem, smem] + [vmem] * 4,
        out_specs=[vmem] * 4,
        scratch_shapes=[
            pltpu.VMEM((2, chunks, span, LANES), jnp.bfloat16),
            pltpu.VMEM((2, chunks, span, LANES), jnp.bfloat16),
            pltpu.VMEM((2, chunks, 2, span, LANES), jnp.bfloat16),
            pltpu.VMEM((2, chunks, 2, span, LANES), jnp.bfloat16),
            pltpu.VMEM((chunks, span, LANES), jnp.float32),
            pltpu.VMEM((chunks, span, LANES), jnp.float32),
            pltpu.SemaphoreType.DMA((2, 2, chunks)),
            pltpu.SemaphoreType.DMA((2, 2, chunks)),
            pltpu.SemaphoreType.DMA((2, chunks)),
            pltpu.SemaphoreType.DMA((2, chunks)),
        ],
        cost_estimate=pl.CostEstimate(
            flops=chunks * pair_flops,
            bytes_accessed=8 * span * width * 2,
            transcendentals=chunks * 4 * VIEW_TOK * 5 * VIEW_TOK,
        ),
        compiler_params=pltpu.CompilerParams(
            collective_id=0, has_side_effects=True, vmem_limit_bytes=40 * 1024 * 1024
        ),
    )(pairs, counts, queries, keys, values, grad_out)


def solution(mesh):
    rows = P(("scene", "view"), None)
    return jax.shard_map(
        body,
        mesh=mesh,
        in_specs=(rows, rows, rows, rows, rows, P(("scene", "view"))),
        out_specs=(rows, rows, rows, rows),
        check_vma=False,
    )
```

time: 148 us -> 61.2 us (0.41)
  waiting for transfers between devices: 54.6 us -> 0 us
  Pallas kernels: 0 us -> 51.6 us
  local copies, waits for them, and re-layouts: 39.1 us -> 8.66 us
  matrix products: 27.5 us -> 0 us
  other arithmetic: 19.1 us -> 0 us
  starting transfers between devices: 6.03 us -> 0 us
    ppermute x4 -> x0, waiting for transfers between devices: 54.6 us -> none  [from_behind(): lax.ppermute(x, axis, [(i, (i + by) % length) for i in range(length)])]
    pallas_call x0 -> x1, Pallas kernels: none -> 51.6 us  [body(): pl.pallas_call(run, name='windowed_attention', out_shape=[jax.ShapeDtypeS...]
    dot_general x12 -> x0, matrix products: 27.5 us -> none  [the longest x2 5.97 us: key_grads(): jnp.einsum('hqk,qhd->khd', weights_b, head_split(d_rows), preferred_eleme...]
    slice x13 -> x0, local copies, waits for them, and re-layouts: 18.2 us -> none  [the longest x2 4.84 us: body(): v_rows = window_kv[1, view * view_rows:(view + 5) * view_rows]]
    another operation x4 -> x0, local copies, waits for them, and re-layouts: 12.9 us -> none  [key_grads(): jnp.stack([key_part.reshape(key_part.shape[0], width), value_part.reshape...]
    another operation x3 -> x0, other arithmetic: 7.9 us -> none
    ppermute x4 -> x0, starting transfers between devices: 6.03 us -> none  [from_behind(): lax.ppermute(x, axis, [(i, (i + by) % length) for i in range(length)])]
    scatter-add x1 -> x0, other arithmetic: 4.61 us -> none  [body(): grad_window.at[:, view * view_rows:(view + 5) * view_rows]]
  transfers between devices with their start and end apart: 4 -> 0, of which waited for: 3 -> 0; matrix products, arithmetic and copies ran while one was open for 11% -> 0% of each run, Pallas kernels for 0% -> 0%
where the time goes in v1:
time: 61.2 us; the launch traced here: 60.9 us
  Pallas kernels  51.6 us (84%)
  local copies, waits for them, and re-layouts  8.66 us (14%)
  between operations  0.66 us (1%)
    pallas_call x1, Pallas kernels, body(): pl.pallas_call(run, name='windowed_attention', out_shape=[jax.ShapeDtypeS...  51.6 us
    unnamed x16, local copies, waits for them, and re-layouts  8.66 us

profile of v1, /device:TPU:0, one launch (start us, length us, event | category | flops | bytes accessed | tf_op | source)
XLA Modules:
  0.0 60.9 jit_solution(14712757270501565355)
XLA Ops:
  0.6 0.0 copy-start
  0.6 1.0 %copy-done = bf16[256,1024]{1,0:T(8,128)(2,1)S(1)} copy-done((bf16[256,1024]{1,0:T(8,128)(2,1)S(1)}, bf16[256,1024]{1,0:T(8,128)(2,1)}, u32[]{:S(2)}) %copy-start) | copy-done | bytes 524312
  1.7 0.0 copy-start.1
  1.7 1.0 %copy-done.1 = bf16[256,1024]{1,0:T(8,128)(2,1)S(1)} copy-done((bf16[256,1024]{1,0:T(8,128)(2,1)S(1)}, bf16[256,1024]{1,0:T(8,128)(2,1)}, u32[]{:S(2)}) %copy-start.1) | copy-done | bytes 524312
  2.7 0.0 copy-start.2
  2.7 1.0 %copy-done.2 = bf16[256,1024]{1,0:T(8,128)(2,1)S(1)} copy-done((bf16[256,1024]{1,0:T(8,128)(2,1)S(1)}, bf16[256,1024]{1,0:T(8,128)(2,1)}, u32[]{:S(2)}) %copy-start.2) | copy-done | bytes 524312
  3.8 0.0 copy-start.3
  3.8 1.0 %copy-done.3 = bf16[256,1024]{1,0:T(8,128)(2,1)S(1)} copy-done((bf16[256,1024]{1,0:T(8,128)(2,1)S(1)}, bf16[256,1024]{1,0:T(8,128)(2,1)}, u32[]{:S(2)}) %copy-start.3) | copy-done | bytes 524312
  4.8 0.0 copy-start.4
  4.8 0.7 %copy-done.4 = s32[2,4]{1,0:T(2,128)S(1)} copy-done((s32[2,4]{1,0:T(2,128)S(1)}, s32[2,4]{1,0:T(2,128)}, u32[]{:S(2)}) %copy-start.4) | copy-done | bytes 56
  5.5 0.0 copy-start.5
  5.5 0.7 %copy-done.5 = s32[2]{0:T(128)S(1)} copy-done((s32[2]{0:T(128)S(1)}, s32[2]{0:T(128)}, u32[]{:S(2)}) %copy-start.5) | copy-done | bytes 32
  6.1 51.6 %windowed_attention.1 = (bf16[256,1024]{1,0:T(8,128)(2,1)S(1)}, bf16[256,1024]{1,0:T(8,128)(2,1)S(1)}, bf16[256,1024]{1,0:T(8,128)(2,1)S(1)}, bf16[256,1024]{1,0:T(8,128)(2,1)S(1)}) custom-call(s32[2,4]{1,0:T(2,128)S(1)} %copy-done.4, s32[2]{0:T(128)S(1)} %copy-done.5, bf16[256,1024]{1,0:T(8,128)(2,1)S(1)} %copy-done, bf16[256,1024]{1,0:T(8,128)(2,1)S(1)} %copy-done.1, ...), custom_call_target="tpu_custom_call" | custom-call | flops 4026531840 | bytes 4194304 | tf_op jit(solution)/shard_map/windowed_attention/pallas_call | solution.py:210
  57.7 0.8 %copy.14 = bf16[256,1024]{1,0:T(8,128)(2,1)} copy(bf16[256,1024]{1,0:T(8,128)(2,1)S(1)} %get-tuple-element.8) | data formatting | bytes 1048576
  58.5 0.8 %copy.15 = bf16[256,1024]{1,0:T(8,128)(2,1)} copy(bf16[256,1024]{1,0:T(8,128)(2,1)S(1)} %get-tuple-element.9) | data formatting | bytes 1048576
  59.3 0.8 %copy.16 = bf16[256,1024]{1,0:T(8,128)(2,1)} copy(bf16[256,1024]{1,0:T(8,128)(2,1)S(1)} %get-tuple-element.10) | data formatting | bytes 1048576
  60.1 0.8 %copy.17 = bf16[256,1024]{1,0:T(8,128)(2,1)} copy(bf16[256,1024]{1,0:T(8,128)(2,1)S(1)} %get-tuple-element.11) | data formatting | bytes 1048576
Async XLA Ops:
  0.6 1.0 %copy-start = (bf16[256,1024]{1,0:T(8,128)(2,1)S(1)}, bf16[256,1024]{1,0:T(8,128)(2,1)}, u32[]{:S(2)}) copy-start(bf16[256,1024]{1,0:T(8,128)(2,1)} %refs_2_.1) | copy-start | bytes 1572868
  1.7 1.0 %copy-start.1 = (bf16[256,1024]{1,0:T(8,128)(2,1)S(1)}, bf16[256,1024]{1,0:T(8,128)(2,1)}, u32[]{:S(2)}) copy-start(bf16[256,1024]{1,0:T(8,128)(2,1)} %refs_3_.1) | copy-start | bytes 1572868
  2.7 1.0 %copy-start.2 = (bf16[256,1024]{1,0:T(8,128)(2,1)S(1)}, bf16[256,1024]{1,0:T(8,128)(2,1)}, u32[]{:S(2)}) copy-start(bf16[256,1024]{1,0:T(8,128)(2,1)} %refs_4_.1) | copy-start | bytes 1572868
  3.8 1.0 %copy-start.3 = (bf16[256,1024]{1,0:T(8,128)(2,1)S(1)}, bf16[256,1024]{1,0:T(8,128)(2,1)}, u32[]{:S(2)}) copy-start(bf16[256,1024]{1,0:T(8,128)(2,1)} %refs_5_.1) | copy-start | bytes 1572868
  4.8 0.7 %copy-start.4 = (s32[2,4]{1,0:T(2,128)S(1)}, s32[2,4]{1,0:T(2,128)}, u32[]{:S(2)}) copy-start(s32[2,4]{1,0:T(2,128)} %refs_0_.1) | copy-start | bytes 100
  5.5 0.7 %copy-start.5 = (s32[2]{0:T(128)S(1)}, s32[2]{0:T(128)}, u32[]{:S(2)}) copy-start(s32[2]{0:T(128)} %refs_1_.1) | copy-start | bytes 28

commit v2 on v1

--- a/solution.py
+++ b/solution.py
@@ -10,6 +10,7 @@
 LANES = 2 * HEAD_DIM
 MASKED = -1e30
 REACH = 2
+VMEM_BYTES = 60 * 1024 * 1024
 
 
 def nt(a, b):
@@ -76,8 +77,10 @@
 
 def kernel(
     size, chunks,
-    pairs, counts, q_ref, k_ref, v_ref, d_ref,
-    a_ref, gq_ref, gk_ref, gv_ref,
+    pairs_hbm, counts_hbm, q_hbm, k_hbm, v_hbm, d_hbm,
+    a_hbm, gq_hbm, gk_hbm, gv_hbm,
+    pairs, counts, q_ref, k_ref, v_ref, d_ref, fetched,
+    a_ref, gq_ref, gk_ref, gv_ref, stored, stored_part,
     k_in, v_in, g_out, g_in, own_k, own_v,
     kv_send, kv_recv, g_send, g_recv,
 ):
@@ -87,11 +90,29 @@
     local_views = span // VIEW_TOK
     views = size * local_views
 
+    fetches = [
+        pltpu.make_async_copy(src, dst, fetched.at[i])
+        for i, (src, dst) in enumerate(
+            (
+                (k_hbm, k_ref),
+                (v_hbm, v_ref),
+                (q_hbm, q_ref),
+                (d_hbm, d_ref),
+                (pairs_hbm, pairs),
+                (counts_hbm, counts),
+            )
+        )
+    ]
+    for fetch in fetches:
+        fetch.start()
+
     barrier = pltpu.get_barrier_semaphore()
     for peer in peers:
         pl.semaphore_signal(
             barrier, inc=1, device_id={"view": peer}, device_id_type=pl.DeviceIdType.MESH
         )
+    for fetch in fetches[:2]:
+        fetch.wait()
     pl.semaphore_wait(barrier, 2)
 
     def columns(c):
@@ -126,6 +147,8 @@
 
     lax.fori_loop(0, chunks, send_all, 0)
 
+    for fetch in fetches[2:]:
+        fetch.wait()
     biases = []
     for view in range(local_views):
         own = me * local_views + view
@@ -170,6 +193,20 @@
 
     lax.fori_loop(0, chunks, work, 0)
 
+    stores = [
+        pltpu.make_async_copy(a_ref, a_hbm, stored.at[0]),
+        pltpu.make_async_copy(gq_ref, gq_hbm, stored.at[1]),
+    ]
+    for copy in stores:
+        copy.start()
+
+    def part_store(c, which):
+        src, dst = ((gk_ref, gk_hbm), (gv_ref, gv_hbm))[which]
+        cols = columns(c)
+        return pltpu.make_async_copy(
+            src.at[:, cols], dst.at[:, cols], stored_part.at[which, c]
+        )
+
     def finish(c, _):
         cols = columns(c)
         for side in (0, 1):
@@ -181,6 +218,7 @@
                 + g_in[1, c, which].astype(jnp.float32)
             )
             result[:, cols] = total.astype(jnp.bfloat16)
+            part_store(c, which).start()
         return 0
 
     lax.fori_loop(0, chunks, finish, 0)
@@ -190,9 +228,25 @@
             for which in (0, 1):
                 kv_copy(c, side, which).wait_send()
             grad_copy(c, side).wait_send()
+        for which in (0, 1):
+            part_store(c, which).wait()
         return 0
 
     lax.fori_loop(0, chunks, drain, 0)
+    for copy in stores:
+        copy.wait()
+
+
+def store(*refs):
+    count = (len(refs) - 1) // 2
+    stored = refs[-1]
+    copies = [
+        pltpu.make_async_copy(refs[i], refs[count + i], stored.at[i]) for i in range(count)
+    ]
+    for copy in copies:
+        copy.start()
+    for copy in copies:
+        copy.wait()
 
 
 def body(queries, keys, values, grad_out, pairs, counts):
@@ -200,20 +254,33 @@
     span, width = queries.shape
     chunks = width // LANES
     assert span == REACH * VIEW_TOK
-    vmem = pl.BlockSpec(memory_space=pltpu.VMEM)
-    smem = pl.BlockSpec(memory_space=pltpu.SMEM)
+    hbm = pl.BlockSpec(memory_space=pltpu.HBM)
 
     def run(*refs):
         kernel(size, chunks, *refs)
 
     pair_flops = 2 * 6 * 2 * 2 * VIEW_TOK * 5 * VIEW_TOK * LANES
-    return pl.pallas_call(
+    block = jax.ShapeDtypeStruct((span, width), jnp.bfloat16)
+    results = pl.pallas_call(
         run,
         name="windowed_attention",
-        out_shape=[jax.ShapeDtypeStruct((span, width), jnp.bfloat16)] * 4,
-        in_specs=[smem, smem] + [vmem] * 4,
-        out_specs=[vmem] * 4,
+        out_shape=[block] * 4,
+        in_specs=[hbm] * 6,
+        out_specs=[hbm] * 4,
         scratch_shapes=[
+            pltpu.SMEM(pairs.shape, pairs.dtype),
+            pltpu.SMEM(counts.shape, counts.dtype),
+            pltpu.VMEM((span, width), jnp.bfloat16),
+            pltpu.VMEM((span, width), jnp.bfloat16),
+            pltpu.VMEM((span, width), jnp.bfloat16),
+            pltpu.VMEM((span, width), jnp.bfloat16),
+            pltpu.SemaphoreType.DMA((6,)),
+            pltpu.VMEM((span, width), jnp.bfloat16),
+            pltpu.VMEM((span, width), jnp.bfloat16),
+            pltpu.VMEM((span, width), jnp.bfloat16),
+            pltpu.VMEM((span, width), jnp.bfloat16),
+            pltpu.SemaphoreType.DMA((2,)),
+            pltpu.SemaphoreType.DMA((2, chunks)),
             pltpu.VMEM((2, chunks, span, LANES), jnp.bfloat16),
             pltpu.VMEM((2, chunks, span, LANES), jnp.bfloat16),
             pltpu.VMEM((2, chunks, 2, span, LANES), jnp.bfloat16),
@@ -231,9 +298,18 @@
             transcendentals=chunks * 4 * VIEW_TOK * 5 * VIEW_TOK,
         ),
         compiler_params=pltpu.CompilerParams(
-            collective_id=0, has_side_effects=True, vmem_limit_bytes=40 * 1024 * 1024
+            collective_id=0, has_side_effects=True, vmem_limit_bytes=VMEM_BYTES
         ),
     )(pairs, counts, queries, keys, values, grad_out)
+    return pl.pallas_call(
+        store,
+        name="store_results",
+        out_shape=[block] * 4,
+        in_specs=[hbm] * 4,
+        out_specs=[hbm] * 4,
+        scratch_shapes=[pltpu.SemaphoreType.DMA((4,))],
+        compiler_params=pltpu.CompilerParams(vmem_limit_bytes=VMEM_BYTES),
+    )(*results)
 
 
 def solution(mesh):

time: 61.2 us -> 117 us (1.91)
  Pallas kernels: 51.6 us -> 116 us
  local copies, waits for them, and re-layouts: 8.66 us -> 0 us
    pallas_call x1 -> x2, Pallas kernels: 51.6 us -> 116 us  [the longest x1 64.7 us: body(): pl.pallas_call(store, name='store_results', out_shape=[block] * 4, in_spe...]
    unnamed x16 -> x0, local copies, waits for them, and re-layouts: 8.66 us -> none
where the time goes in v2:
time: 117 us
  Pallas kernels  116 us (99%)
    pallas_call x1, Pallas kernels, body(): pl.pallas_call(store, name='store_results', out_shape=[block] * 4, in_spe...  64.7 us
    pallas_call x1, Pallas kernels, body(): pl.pallas_call(run, name='windowed_attention', out_shape=[block] * 4, in_...  51.7 us

profile of v2, /device:TPU:0, one launch (start us, length us, event | category | flops | bytes accessed | tf_op | source)
XLA Modules:
  0.0 117.0 jit_solution(4697905771580113458)
XLA Ops:
  0.6 51.7 %windowed_attention.1 = (bf16[256,1024]{1,0:T(8,128)(2,1)}, bf16[256,1024]{1,0:T(8,128)(2,1)}, bf16[256,1024]{1,0:T(8,128)(2,1)}, bf16[256,1024]{1,0:T(8,128)(2,1)}) custom-call(s32[2,4]{1,0:T(2,128)} %refs_0_.1, s32[2]{0:T(128)} %refs_1_.1, bf16[256,1024]{1,0:T(8,128)(2,1)} %refs_2_.1, bf16[256,1024]{1,0:T(8,128)(2,1)} %refs_3_.1, ...), custom_call_target="tpu_custom_call" | custom-call | flops 4026531840 | bytes 4194304 | tf_op jit(solution)/shard_map/windowed_attention/pallas_call | solution.py:264
  52.3 64.7 %store_results.1 = (bf16[256,1024]{1,0:T(8,128)(2,1)}, bf16[256,1024]{1,0:T(8,128)(2,1)}, bf16[256,1024]{1,0:T(8,128)(2,1)}, bf16[256,1024]{1,0:T(8,128)(2,1)}) custom-call(bf16[256,1024]{1,0:T(8,128)(2,1)} %get-tuple-element.8.refs_0_, bf16[256,1024]{1,0:T(8,128)(2,1)} %get-tuple-element.9.refs_1_, bf16[256,1024]{1,0:T(8,128)(2,1)} %get-tuple-element.10.refs_2_, ...), custom_call_target="tpu_custom_call" | custom-call | tf_op jit(solution)/shard_map/store_results/pallas_call | solution.py:304

commit v3 on v2

--- a/solution.py
+++ b/solution.py
@@ -1,3 +1,5 @@
+import functools
+
 import jax
 import jax.numpy as jnp
 from jax import lax
@@ -237,15 +239,17 @@
         copy.wait()
 
 
-def store(*refs):
-    count = (len(refs) - 1) // 2
-    stored = refs[-1]
-    copies = [
-        pltpu.make_async_copy(refs[i], refs[count + i], stored.at[i]) for i in range(count)
-    ]
-    for copy in copies:
-        copy.start()
-    for copy in copies:
+def store(count, *refs):
+    sources, targets, held = refs[:count], refs[count : 2 * count], refs[2 * count : 3 * count]
+    loaded, stored = refs[3 * count :]
+    loads = [pltpu.make_async_copy(sources[i], held[i], loaded.at[i]) for i in range(count)]
+    stores = [pltpu.make_async_copy(held[i], targets[i], stored.at[i]) for i in range(count)]
+    for load in loads:
+        load.start()
+    for i in range(count):
+        loads[i].wait()
+        stores[i].start()
+    for copy in stores:
         copy.wait()
 
 
@@ -302,12 +306,13 @@
         ),
     )(pairs, counts, queries, keys, values, grad_out)
     return pl.pallas_call(
-        store,
+        functools.partial(store, 4),
         name="store_results",
         out_shape=[block] * 4,
         in_specs=[hbm] * 4,
         out_specs=[hbm] * 4,
-        scratch_shapes=[pltpu.SemaphoreType.DMA((4,))],
+        scratch_shapes=[pltpu.VMEM((span, width), jnp.bfloat16)] * 4
+        + [pltpu.SemaphoreType.DMA((4,)), pltpu.SemaphoreType.DMA((4,))],
         compiler_params=pltpu.CompilerParams(vmem_limit_bytes=VMEM_BYTES),
     )(*results)
 

time: 117 us -> 54.9 us (0.47)
  Pallas kernels: 116 us -> 54.1 us
    pallas_call x1, Pallas kernels: 64.7 us -> 2.42 us  [body(): pl.pallas_call(functools.partial(store, 4), name='store_results', out_sha...]
where the time goes in v3:
time: 54.9 us; the launch traced here: 54.7 us
  Pallas kernels  54.1 us (99%)
  between operations  0.64 us (1%)
    pallas_call x1, Pallas kernels, body(): pl.pallas_call(run, name='windowed_attention', out_shape=[block] * 4, in_...  51.7 us
    pallas_call x1, Pallas kernels, body(): pl.pallas_call(functools.partial(store, 4), name='store_results', out_sha...  2.42 us

profile of v3, /device:TPU:0, one launch (start us, length us, event | category | flops | bytes accessed | tf_op | source)
XLA Modules:
  0.0 54.7 jit_solution(17643535617702645314)
XLA Ops:
  0.6 51.7 %windowed_attention.1 = (bf16[256,1024]{1,0:T(8,128)(2,1)}, bf16[256,1024]{1,0:T(8,128)(2,1)}, bf16[256,1024]{1,0:T(8,128)(2,1)}, bf16[256,1024]{1,0:T(8,128)(2,1)}) custom-call(s32[2,4]{1,0:T(2,128)} %refs_0_.1, s32[2]{0:T(128)} %refs_1_.1, bf16[256,1024]{1,0:T(8,128)(2,1)} %refs_2_.1, bf16[256,1024]{1,0:T(8,128)(2,1)} %refs_3_.1, ...), custom_call_target="tpu_custom_call" | custom-call | flops 4026531840 | bytes 4194304 | tf_op jit(solution)/shard_map/windowed_attention/pallas_call | solution.py:268
  52.3 2.4 %store_results.1 = (bf16[256,1024]{1,0:T(8,128)(2,1)}, bf16[256,1024]{1,0:T(8,128)(2,1)}, bf16[256,1024]{1,0:T(8,128)(2,1)}, bf16[256,1024]{1,0:T(8,128)(2,1)}) custom-call(bf16[256,1024]{1,0:T(8,128)(2,1)} %get-tuple-element.8.refs_0_, bf16[256,1024]{1,0:T(8,128)(2,1)} %get-tuple-element.9.refs_1_, bf16[256,1024]{1,0:T(8,128)(2,1)} %get-tuple-element.10.refs_2_, ...), custom_call_target="tpu_custom_call" | custom-call | tf_op jit(solution)/shard_map/store_results/pallas_call | solution.py:308

commit v4 on v3

--- a/solution.py
+++ b/solution.py
@@ -81,9 +81,9 @@
     size, chunks,
     pairs_hbm, counts_hbm, q_hbm, k_hbm, v_hbm, d_hbm,
     a_hbm, gq_hbm, gk_hbm, gv_hbm,
-    pairs, counts, q_ref, k_ref, v_ref, d_ref, fetched,
+    pairs, counts, q_ref, d_ref, kv_ref, fetched, kv_fetched,
     a_ref, gq_ref, gk_ref, gv_ref, stored, stored_part,
-    k_in, v_in, g_out, g_in, own_k, own_v,
+    kv_in, g_out, g_in, own_k, own_v,
     kv_send, kv_recv, g_send, g_recv,
 ):
     me = lax.axis_index("view")
@@ -92,12 +92,24 @@
     local_views = span // VIEW_TOK
     views = size * local_views
 
+    def columns(c):
+        return pl.ds(pl.multiple_of(c * LANES, LANES), LANES)
+
+    def kv_fetch(c, which):
+        return pltpu.make_async_copy(
+            (k_hbm, v_hbm)[which].at[:, columns(c)], kv_ref.at[c, which], kv_fetched.at[which, c]
+        )
+
+    def fetch_all(c, _):
+        for which in (0, 1):
+            kv_fetch(c, which).start()
+        return 0
+
+    lax.fori_loop(0, chunks, fetch_all, 0)
     fetches = [
         pltpu.make_async_copy(src, dst, fetched.at[i])
         for i, (src, dst) in enumerate(
             (
-                (k_hbm, k_ref),
-                (v_hbm, v_ref),
                 (q_hbm, q_ref),
                 (d_hbm, d_ref),
                 (pairs_hbm, pairs),
@@ -113,20 +125,14 @@
         pl.semaphore_signal(
             barrier, inc=1, device_id={"view": peer}, device_id_type=pl.DeviceIdType.MESH
         )
-    for fetch in fetches[:2]:
-        fetch.wait()
     pl.semaphore_wait(barrier, 2)
 
-    def columns(c):
-        return pl.ds(pl.multiple_of(c * LANES, LANES), LANES)
-
-    def kv_copy(c, side, which):
-        src, dst = ((k_ref, k_in), (v_ref, v_in))[which]
+    def kv_copy(c, side):
         return pltpu.make_async_remote_copy(
-            src_ref=src.at[:, columns(c)],
-            dst_ref=dst.at[1 - side, c],
-            send_sem=kv_send.at[side, which, c],
-            recv_sem=kv_recv.at[1 - side, which, c],
+            src_ref=kv_ref.at[c],
+            dst_ref=kv_in.at[1 - side, c],
+            send_sem=kv_send.at[side, c],
+            recv_sem=kv_recv.at[1 - side, c],
             device_id={"view": peers[side]},
             device_id_type=pl.DeviceIdType.MESH,
         )
@@ -143,13 +149,14 @@
 
     def send_all(c, _):
         for which in (0, 1):
-            for side in (0, 1):
-                kv_copy(c, side, which).start()
+            kv_fetch(c, which).wait()
+        for side in (0, 1):
+            kv_copy(c, side).start()
         return 0
 
     lax.fori_loop(0, chunks, send_all, 0)
 
-    for fetch in fetches[2:]:
+    for fetch in fetches:
         fetch.wait()
     biases = []
     for view in range(local_views):
@@ -162,12 +169,13 @@
         )
 
     def work(c, _):
-        for which in (0, 1):
-            for side in (0, 1):
-                kv_copy(c, side, which).wait_recv()
+        for side in (0, 1):
+            kv_copy(c, side).wait_recv()
         cols = columns(c)
-        k_all = jnp.concatenate([k_in[0, c], k_ref[:, cols], k_in[1, c]], axis=0)
-        v_all = jnp.concatenate([v_in[0, c], v_ref[:, cols], v_in[1, c]], axis=0)
+        k_all, v_all = (
+            jnp.concatenate([kv_in[0, c, which], kv_ref[c, which], kv_in[1, c, which]], axis=0)
+            for which in (0, 1)
+        )
         sums = [[None] * (3 * local_views), [None] * (3 * local_views)]
         for view in range(local_views):
             rows = slice(view * VIEW_TOK, (view + 1) * VIEW_TOK)
@@ -227,8 +235,7 @@
 
     def drain(c, _):
         for side in (0, 1):
-            for which in (0, 1):
-                kv_copy(c, side, which).wait_send()
+            kv_copy(c, side).wait_send()
             grad_copy(c, side).wait_send()
         for which in (0, 1):
             part_store(c, which).wait()
@@ -276,23 +283,22 @@
             pltpu.SMEM(counts.shape, counts.dtype),
             pltpu.VMEM((span, width), jnp.bfloat16),
             pltpu.VMEM((span, width), jnp.bfloat16),
-            pltpu.VMEM((span, width), jnp.bfloat16),
-            pltpu.VMEM((span, width), jnp.bfloat16),
-            pltpu.SemaphoreType.DMA((6,)),
+            pltpu.VMEM((chunks, 2, span, LANES), jnp.bfloat16),
+            pltpu.SemaphoreType.DMA((4,)),
+            pltpu.SemaphoreType.DMA((2, chunks)),
             pltpu.VMEM((span, width), jnp.bfloat16),
             pltpu.VMEM((span, width), jnp.bfloat16),
             pltpu.VMEM((span, width), jnp.bfloat16),
             pltpu.VMEM((span, width), jnp.bfloat16),
             pltpu.SemaphoreType.DMA((2,)),
             pltpu.SemaphoreType.DMA((2, chunks)),
-            pltpu.VMEM((2, chunks, span, LANES), jnp.bfloat16),
-            pltpu.VMEM((2, chunks, span, LANES), jnp.bfloat16),
+            pltpu.VMEM((2, chunks, 2, span, LANES), jnp.bfloat16),
             pltpu.VMEM((2, chunks, 2, span, LANES), jnp.bfloat16),
             pltpu.VMEM((2, chunks, 2, span, LANES), jnp.bfloat16),
             pltpu.VMEM((chunks, span, LANES), jnp.float32),
             pltpu.VMEM((chunks, span, LANES), jnp.float32),
-            pltpu.SemaphoreType.DMA((2, 2, chunks)),
-            pltpu.SemaphoreType.DMA((2, 2, chunks)),
+            pltpu.SemaphoreType.DMA((2, chunks)),
+            pltpu.SemaphoreType.DMA((2, chunks)),
             pltpu.SemaphoreType.DMA((2, chunks)),
             pltpu.SemaphoreType.DMA((2, chunks)),
         ],

time: 54.9 us -> 54.4 us (level)
  no operation moved by 1% of the time
where the time goes in v4:
time: 54.4 us; the launch traced here: 54.2 us
  Pallas kernels  53.6 us (99%)
  between operations  0.64 us (1%)
    pallas_call x1, Pallas kernels, body(): pl.pallas_call(run, name='windowed_attention', out_shape=[block] * 4, in_...  51.2 us
    pallas_call x1, Pallas kernels, body(): pl.pallas_call(functools.partial(store, 4), name='store_results', out_sha...  2.42 us

profile of v4, /device:TPU:0, one launch (start us, length us, event | category | flops | bytes accessed | tf_op | source)
XLA Modules:
  0.0 54.2 jit_solution(7091698788021577161)
XLA Ops:
  0.6 51.2 %windowed_attention.1 = (bf16[256,1024]{1,0:T(8,128)(2,1)}, bf16[256,1024]{1,0:T(8,128)(2,1)}, bf16[256,1024]{1,0:T(8,128)(2,1)}, bf16[256,1024]{1,0:T(8,128)(2,1)}) custom-call(s32[2,4]{1,0:T(2,128)} %refs_0_.1, s32[2]{0:T(128)} %refs_1_.1, bf16[256,1024]{1,0:T(8,128)(2,1)} %refs_2_.1, bf16[256,1024]{1,0:T(8,128)(2,1)} %refs_3_.1, ...), custom_call_target="tpu_custom_call" | custom-call | flops 4026531840 | bytes 4194304 | tf_op jit(solution)/shard_map/windowed_attention/pallas_call | solution.py:275
  51.8 2.4 %store_results.1 = (bf16[256,1024]{1,0:T(8,128)(2,1)}, bf16[256,1024]{1,0:T(8,128)(2,1)}, bf16[256,1024]{1,0:T(8,128)(2,1)}, bf16[256,1024]{1,0:T(8,128)(2,1)}) custom-call(bf16[256,1024]{1,0:T(8,128)(2,1)} %get-tuple-element.8.refs_0_, bf16[256,1024]{1,0:T(8,128)(2,1)} %get-tuple-element.9.refs_1_, bf16[256,1024]{1,0:T(8,128)(2,1)} %get-tuple-element.10.refs_2_, ...), custom_call_target="tpu_custom_call" | custom-call | tf_op jit(solution)/shard_map/store_results/pallas_call | solution.py:314

commit v5 on v4

--- a/solution.py
+++ b/solution.py
@@ -133,7 +133,7 @@
             dst_ref=kv_in.at[1 - side, c],
             send_sem=kv_send.at[side, c],
             recv_sem=kv_recv.at[1 - side, c],
-            device_id={"view": peers[side]},
+            device_id={"view": lax.rem(me + size - 1 + 2 * side, size)},
             device_id_type=pl.DeviceIdType.MESH,
         )
 
@@ -150,8 +150,8 @@
     def send_all(c, _):
         for which in (0, 1):
             kv_fetch(c, which).wait()
-        for side in (0, 1):
-            kv_copy(c, side).start()
+        for turn in (0, 1):
+            kv_copy(c, lax.rem(me + turn, 2)).start()
         return 0
 
     lax.fori_loop(0, chunks, send_all, 0)

time: 54.4 us -> 54.4 us (level)
  no operation moved by 1% of the time
where the time goes in v5:
time: 54.4 us; the launch traced here: 54.2 us
  Pallas kernels  53.6 us (99%)
  between operations  0.64 us (1%)
    pallas_call x1, Pallas kernels, body(): pl.pallas_call(run, name='windowed_attention', out_shape=[block] * 4, in_...  51.2 us
    pallas_call x1, Pallas kernels, body(): pl.pallas_call(functools.partial(store, 4), name='store_results', out_sha...  2.42 us

profile of v5, /device:TPU:0, one launch (start us, length us, event | category | flops | bytes accessed | tf_op | source)
XLA Modules:
  0.0 54.2 jit_solution(12573795627322607229)
XLA Ops:
  0.6 51.2 %windowed_attention.1 = (bf16[256,1024]{1,0:T(8,128)(2,1)}, bf16[256,1024]{1,0:T(8,128)(2,1)}, bf16[256,1024]{1,0:T(8,128)(2,1)}, bf16[256,1024]{1,0:T(8,128)(2,1)}) custom-call(s32[2,4]{1,0:T(2,128)} %refs_0_.1, s32[2]{0:T(128)} %refs_1_.1, bf16[256,1024]{1,0:T(8,128)(2,1)} %refs_2_.1, bf16[256,1024]{1,0:T(8,128)(2,1)} %refs_3_.1, ...), custom_call_target="tpu_custom_call" | custom-call | flops 4026531840 | bytes 4194304 | tf_op jit(solution)/shard_map/windowed_attention/pallas_call | solution.py:275
  51.8 2.4 %store_results.1 = (bf16[256,1024]{1,0:T(8,128)(2,1)}, bf16[256,1024]{1,0:T(8,128)(2,1)}, bf16[256,1024]{1,0:T(8,128)(2,1)}, bf16[256,1024]{1,0:T(8,128)(2,1)}) custom-call(bf16[256,1024]{1,0:T(8,128)(2,1)} %get-tuple-element.8.refs_0_, bf16[256,1024]{1,0:T(8,128)(2,1)} %get-tuple-element.9.refs_1_, bf16[256,1024]{1,0:T(8,128)(2,1)} %get-tuple-element.10.refs_2_, ...), custom_call_target="tpu_custom_call" | custom-call | tf_op jit(solution)/shard_map/store_results/pallas_call | solution.py:314

commit v6 on v5

--- a/solution.py
+++ b/solution.py
@@ -249,13 +249,21 @@
 def store(count, *refs):
     sources, targets, held = refs[:count], refs[count : 2 * count], refs[2 * count : 3 * count]
     loaded, stored = refs[3 * count :]
-    loads = [pltpu.make_async_copy(sources[i], held[i], loaded.at[i]) for i in range(count)]
-    stores = [pltpu.make_async_copy(held[i], targets[i], stored.at[i]) for i in range(count)]
+    half = held[0].shape[0] // 2
+    pieces = [(i, pl.ds(part * half, half)) for i in range(count) for part in (0, 1)]
+    loads = [
+        pltpu.make_async_copy(sources[i].at[rows], held[i].at[rows], loaded.at[n])
+        for n, (i, rows) in enumerate(pieces)
+    ]
+    stores = [
+        pltpu.make_async_copy(held[i].at[rows], targets[i].at[rows], stored.at[n])
+        for n, (i, rows) in enumerate(pieces)
+    ]
     for load in loads:
         load.start()
-    for i in range(count):
-        loads[i].wait()
-        stores[i].start()
+    for load, copy in zip(loads, stores):
+        load.wait()
+        copy.start()
     for copy in stores:
         copy.wait()
 
@@ -318,7 +326,7 @@
         in_specs=[hbm] * 4,
         out_specs=[hbm] * 4,
         scratch_shapes=[pltpu.VMEM((span, width), jnp.bfloat16)] * 4
-        + [pltpu.SemaphoreType.DMA((4,)), pltpu.SemaphoreType.DMA((4,))],
+        + [pltpu.SemaphoreType.DMA((8,)), pltpu.SemaphoreType.DMA((8,))],
         compiler_params=pltpu.CompilerParams(vmem_limit_bytes=VMEM_BYTES),
     )(*results)
 

time: 54.4 us -> 54.4 us (level)
  no operation moved by 1% of the time
where the time goes in v6:
time: 54.4 us; the launch traced here: 54.2 us
  Pallas kernels  53.6 us (99%)
  between operations  0.64 us (1%)
    pallas_call x1, Pallas kernels, body(): pl.pallas_call(run, name='windowed_attention', out_shape=[block] * 4, in_...  51.2 us
    pallas_call x1, Pallas kernels, body(): pl.pallas_call(functools.partial(store, 4), name='store_results', out_sha...  2.4 us

profile of v6, /device:TPU:0, one launch (start us, length us, event | category | flops | bytes accessed | tf_op | source)
XLA Modules:
  0.0 54.2 jit_solution(2454597620392246160)
XLA Ops:
  0.6 51.2 %windowed_attention.1 = (bf16[256,1024]{1,0:T(8,128)(2,1)}, bf16[256,1024]{1,0:T(8,128)(2,1)}, bf16[256,1024]{1,0:T(8,128)(2,1)}, bf16[256,1024]{1,0:T(8,128)(2,1)}) custom-call(s32[2,4]{1,0:T(2,128)} %refs_0_.1, s32[2]{0:T(128)} %refs_1_.1, bf16[256,1024]{1,0:T(8,128)(2,1)} %refs_2_.1, bf16[256,1024]{1,0:T(8,128)(2,1)} %refs_3_.1, ...), custom_call_target="tpu_custom_call" | custom-call | flops 4026531840 | bytes 4194304 | tf_op jit(solution)/shard_map/windowed_attention/pallas_call | solution.py:283
  51.8 2.4 %store_results.1 = (bf16[256,1024]{1,0:T(8,128)(2,1)}, bf16[256,1024]{1,0:T(8,128)(2,1)}, bf16[256,1024]{1,0:T(8,128)(2,1)}, bf16[256,1024]{1,0:T(8,128)(2,1)}) custom-call(bf16[256,1024]{1,0:T(8,128)(2,1)} %get-tuple-element.8.refs_0_, bf16[256,1024]{1,0:T(8,128)(2,1)} %get-tuple-element.9.refs_1_, bf16[256,1024]{1,0:T(8,128)(2,1)} %get-tuple-element.10.refs_2_, ...), custom_call_target="tpu_custom_call" | custom-call | tf_op jit(solution)/shard_map/store_results/pallas_call | solution.py:322
